TPU v7x, 32 devices: a whole 2x2x4 slice. The times are simulated.
32 devices in a mesh: parts: 2 (over y), ctx: 16 (over z, x, core).
Axes of the slice: x: 2, y: 2, z: 4, core: 2. Of those that a mesh axis runs over, the one named last changes fastest.
Arguments:
- tokens: bfloat16 [4096, 1024], P(('parts', 'ctx')), parts along dimension 0, may hold values from -8 to 8
- boundary: int32 [4096], P(('parts', 'ctx')), parts along dimension 0, may hold values from 0 to 1, as said below
- w_qkv_full: bfloat16 [1024, 1536], replicated, may hold values from -2 to 2
- w_out_full: bfloat16 [512, 1024], replicated, may hold values from -2 to 2
- w_qkv_short: bfloat16 [1024, 1536], replicated, may hold values from -2 to 2
- w_out_short: bfloat16 [512, 1024], replicated, may hold values from -1.5 to 1.5
Outputs:
- upsampled: bfloat16 [4096, 1024], P(('parts', 'ctx')), parts along dimension 0
There are 2 independent parts, one for each index of `parts`. A program takes and returns all parts, laid end to end along the dimension named above; an argument that names none is the same for every part. Nothing has to cross between parts.
Inputs may be any that keep to these rules, and one draw needn't show every extreme that they name: `boundary`: the first token of the sequence is marked. The tokens of one device hold 16, 32 or 64 marks; in each aligned group of four devices these counts are 64, 32, 16, 16 in some order, so that all marks together number 512. The marks in the tokens of devices 0 to d - 1 number between (d - 1) * 32 and (d + 1) * 32; both bounds and the count 64 are reached in every draw.
All inputs are finite; a program needn't handle non-finite values.
Results may differ from a plain program's by a relative error of at most 0.012.
The roundings to bfloat16 on the way count: a program that leaves them out, or rounds other values in their place, can miss the bound.
Values may be sent and summed in bfloat16 or wider, within the bound.
A program may use at most 128 MiB of HBM per device.

v0:
```python
import jax
import jax.numpy as jnp
from jax import lax
from jax.sharding import PartitionSpec as P

HEADS = 8
HEAD_DIM = 64
WINDOW = 128


EPSILON = 1e-06
MASKED = -1e30
FARAWAY = 1 << 30
KEY_BLOCK = 2048


def from_behind(block, axis, distance):
    devices = range(lax.axis_size(axis))
    route = [(i - distance, i) for i in devices if i - distance in devices]
    return lax.ppermute(block, axis, route)


def normalize(matrix):
    values = matrix.astype(jnp.float32)
    inverse = lax.rsqrt(jnp.mean(values * values, axis=-1, keepdims=True) + EPSILON)
    return (values * inverse).astype(jnp.bfloat16)


def window_attend(queries, key_block, value_block, allowed):
    row_count = queries.shape[0]
    key_count = key_block.shape[0]
    query_heads = queries.reshape(row_count, HEADS, HEAD_DIM)
    key_heads = key_block.reshape(key_count, HEADS, HEAD_DIM)
    value_heads = value_block.reshape(key_count, HEADS, HEAD_DIM)
    scores = jnp.einsum(
        "qhd,khd->hqk", query_heads, key_heads, preferred_element_type=jnp.float32
    ) * HEAD_DIM ** (-0.5)
    scores = jnp.where(allowed[None], scores, MASKED)
    highest = jnp.max(scores, axis=-1, keepdims=True)
    expsum = jnp.where(allowed[None], jnp.exp(scores - highest), 0.0)
    row_total = jnp.sum(expsum, axis=-1)
    mixed_heads = jnp.einsum(
        "hqk,khd->qhd", expsum.astype(jnp.bfloat16), value_heads, preferred_element_type=jnp.float32
    )
    mixed_heads = mixed_heads / row_total.transpose(1, 0)[:, :, None]
    return mixed_heads.reshape(row_count, HEADS * HEAD_DIM).astype(jnp.bfloat16)


def absorb(state_carry, query_heads, query_place, key_values, key_place):
    row_max, row_total, running = state_carry
    inner_width = HEADS * HEAD_DIM
    key_count = key_values.shape[0]
    for block_start in range(0, key_count, KEY_BLOCK):
        block_end = min(key_count, block_start + KEY_BLOCK)
        key_slice = key_values[block_start:block_end]
        places = key_place[block_start:block_end]
        key_heads = key_slice[:, :inner_width].reshape(block_end - block_start, HEADS, HEAD_DIM)
        value_heads = key_slice[:, inner_width:].reshape(block_end - block_start, HEADS, HEAD_DIM)
        scores = jnp.einsum(
            "qhd,khd->hqk", query_heads, key_heads, preferred_element_type=jnp.float32
        ) * HEAD_DIM ** (-0.5)
        allowed = places[None, :] <= query_place[:, None]
        scores = jnp.where(allowed[None], scores, MASKED)
        new_max = jnp.maximum(row_max, jnp.max(scores, axis=-1, keepdims=True))
        expsum = jnp.where(allowed[None], jnp.exp(scores - new_max), 0.0)
        fading = jnp.exp(row_max - new_max)
        row_total = row_total * fading + jnp.sum(expsum, axis=-1, keepdims=True)
        running = running * fading + jnp.einsum(
            "hqk,khd->hqd",
            expsum.astype(jnp.bfloat16),
            value_heads,
            preferred_element_type=jnp.float32,
        )
        row_max = new_max
    return (row_max, row_total, running)


def empty_state(row_count):
    return (
        jnp.full((HEADS, row_count, 1), MASKED, jnp.float32),
        jnp.zeros((HEADS, row_count, 1), jnp.float32),
        jnp.zeros((HEADS, row_count, HEAD_DIM), jnp.float32),
    )


def finish_state(state_carry):
    row_max, row_total, running = state_carry
    mixed_heads = running / row_total
    return (
        mixed_heads.transpose(1, 0, 2)
        .reshape(running.shape[1], HEADS * HEAD_DIM)
        .astype(jnp.bfloat16)
    )


def shards(tokens, boundary, w_qkv_full, w_out_full, w_qkv_short, w_out_short):
    length = tokens.shape[0]
    inner_width = HEADS * HEAD_DIM
    device = lax.axis_index("ctx")
    devices = lax.axis_size("ctx")
    capacity = length // 2
    normed = normalize(tokens)
    packed = jnp.dot(normed, w_qkv_full, preferred_element_type=jnp.float32).astype(jnp.bfloat16)
    key_value = packed[:, inner_width:]
    earlier = from_behind(key_value, "ctx", 1)
    beside_all = jnp.concatenate([earlier, key_value], axis=0)
    query_pos = device * length + jnp.arange(length, dtype=jnp.int32)
    key_pos = device * length - length + jnp.arange(2 * length, dtype=jnp.int32)
    allowed = (
        (key_pos[None, :] <= query_pos[:, None])
        & (key_pos[None, :] > query_pos[:, None] - WINDOW)
        & (key_pos[None, :] >= 0)
    )
    mixed_full = window_attend(
        packed[:, :inner_width], beside_all[:, :inner_width], beside_all[:, inner_width:], allowed
    )
    stream = (
        tokens.astype(jnp.float32)
        + jnp.dot(mixed_full, w_out_full, preferred_element_type=jnp.float32)
    ).astype(jnp.bfloat16)
    local_segment = jnp.cumsum(boundary) - 1
    starts = jnp.sum(boundary)
    slot_ids = jnp.arange(capacity, dtype=jnp.int32)
    gather_matrix = (slot_ids[:, None] == local_segment[None, :]).astype(jnp.bfloat16)
    partial_value = jnp.dot(gather_matrix, stream, preferred_element_type=jnp.float32)
    leading = (local_segment == -1).astype(jnp.bfloat16)[None, :]
    lead_sum = jnp.dot(leading, stream, preferred_element_type=jnp.float32)
    lead_size = jnp.sum(leading.astype(jnp.float32), axis=1)
    tail_sum, tail_size = from_behind((lead_sum, lead_size), "ctx", -1)
    closing = (slot_ids == starts - 1).astype(jnp.float32)
    seg_sizes = jnp.sum(gather_matrix.astype(jnp.float32), axis=1) + closing * tail_size[0]
    totals = partial_value + closing[:, None] * tail_sum
    pooled = (totals / jnp.maximum(seg_sizes, 1.0)[:, None]).astype(jnp.bfloat16)
    every_count = lax.all_gather(starts.reshape(1), "ctx", axis=0, tiled=True)
    device_ids = jnp.arange(devices, dtype=jnp.int32)
    every_first = jnp.cumsum(every_count) - every_count
    first_slot = jnp.sum(jnp.where(device_ids < device, every_count, 0))
    global_slot = first_slot + slot_ids
    slot_live = slot_ids < starts
    ragged_packed = jnp.dot(
        normalize(pooled), w_qkv_short, preferred_element_type=jnp.float32
    ).astype(jnp.bfloat16)
    query_place = jnp.where(slot_live, global_slot, FARAWAY)
    query_heads = ragged_packed[:, :inner_width].reshape(capacity, HEADS, HEAD_DIM)
    key_piece = lax.all_gather(ragged_packed[:, inner_width:], "ctx", axis=0, tiled=True)
    key_index = jnp.arange(key_piece.shape[0], dtype=jnp.int32)
    owner_ids = key_index // capacity
    within = key_index - owner_ids * capacity
    owner_match = owner_ids[:, None] == device_ids[None, :]
    owner_first = jnp.sum(jnp.where(owner_match, every_first[None, :], 0), axis=1)
    owner_count = jnp.sum(jnp.where(owner_match, every_count[None, :], 0), axis=1)
    key_place = jnp.where(within < owner_count, owner_first + within, FARAWAY)
    folded = absorb(empty_state(capacity), query_heads, query_place, key_piece, key_place)
    short_out = (
        pooled.astype(jnp.float32)
        + jnp.dot(finish_state(folded), w_out_short, preferred_element_type=jnp.float32)
    ).astype(jnp.bfloat16)
    before_closing = (slot_ids == starts - 2).astype(jnp.float32)
    last_two = jnp.stack([closing, before_closing], axis=0).astype(jnp.bfloat16)
    tail_rows = jnp.dot(last_two, short_out, preferred_element_type=jnp.float32).astype(
        jnp.bfloat16
    )
    before = from_behind(tail_rows, "ctx", 1).astype(jnp.float32)
    shifted_matrix = (slot_ids[:, None] == (local_segment - 1)[None, :]).astype(jnp.bfloat16)
    lifted = lax.dot_general(
        shifted_matrix, short_out, (((0,), (0,)), ((), ())), preferred_element_type=jnp.float32
    )
    first_run = (local_segment == 0).astype(jnp.float32).reshape(length, 1)
    lifted = (
        lifted
        + first_run * before[0][None, :]
        + leading.astype(jnp.float32).reshape(length, 1) * before[1][None, :]
    )
    return (stream.astype(jnp.float32) + lifted).astype(jnp.bfloat16)


def solution(mesh):
    return jax.shard_map(
        shards,
        mesh=mesh,
        in_specs=(P(("parts", "ctx"), None), P(("parts", "ctx")), P(), P(), P(), P()),
        out_specs=P(("parts", "ctx"), None),
        check_vma=False,
    )
```

profile of v0, /device:TPU:8, one launch (start us, length us, event | category | flops | bytes accessed | tf_op | source)
XLA Modules:
  0.0 115.6 jit_solution(6202416924744937240)
XLA Ops:
  6.5 1.2 %fusion.21 = f32[128]{0:T(128)S(1)} fusion(bf16[128,1024]{1,0:T(8,128)(2,1)} %param.6), kind=kLoop, calls=%fused_computation.32 | loop fusion | flops 393088 | bytes 262656 | tf_op jit(solution)/shard_map/reduce_sum | solution.py:25
  8.5 1.6 %convolution_convert_fusion = bf16[128,1536]{1,0:T(8,128)(2,1)S(1)} fusion(bf16[1024,1536]{1,0:T(8,128)(2,1)S(1)} %copy-done, bf16[128,1024]{1,0:T(8,128)(2,1)} %param.6, f32[128]{0:T(128)S(1)} %add_rsqrt_fusion.1), kind=kOutput, calls=%fused_computation.1 | convolution fusion | flops 403243008 | bytes 3801600 | tf_op jit(solution)/shard_map/dot_general | solution.py:103
  10.8 1.9 %collective-permute-start = (bf16[128,1024]{1,0:T(8,128)(2,1)}, bf16[128,1024]{1,0:T(8,128)(2,1)}, u32[]{:S(2)}, u32[]{:S(2)}) collective-permute-start(bf16[128,1024]{1,0:T(8,128)(2,1)} %slice.40), channel_id=1, source_target_pairs={{0,1},{1,2},{2,3},{3,4},{4,5},{5,6},{6,7},{7,8},{8,9},{9,10},{10,1... | collective-permute-start | bytes 786440 | tf_op jit(solution)/shard_map/ppermute | solution.py:20
  13.5 1.6 %reduce-window.14 = s32[128,1]{1,0:T(8,128)} reduce-window(s32[128,1]{1,0:T(8,128)} %copy.27, s32[]{:T(128)} %constant.64.clone.1), window={size=128x1 pad=127_0x0_0}, to_apply=%region_3.4 | reduce-window | flops 16256 | bytes 1028 | tf_op jit(solution)/shard_map/reduce-window
  15.1 1.5 %convert_reduce_fusion = f32[]{:T(128)} fusion(s32[128,1]{1,0:T(8,128)} %reduce-window.14), kind=kLoop, calls=%fused_computation.54 | loop fusion | flops 639 | bytes 516 | tf_op jit(solution)/shard_map/reduce_sum | solution.py:128
  16.6 4.5 %collective-permute-start.2 = (f32[1]{0:T(128)}, f32[1]{0:T(128)}, u32[]{:S(2)}, u32[]{:S(2)}) collective-permute-start(f32[1]{0:T(128)} %bitcast.10), channel_id=1, source_target_pairs={{1,0},{2,1},{3,2},{4,3},{5,4},{6,5},{7,6},{8,7},{9,8},{10,9},{11,1... | collective-permute-start | bytes 20 | tf_op jit(solution)/shard_map/ppermute | solution.py:20
  22.3 0.9 add_reduce_fusion
  26.0 1.0 copy.25
  27.0 1.4 %and_and_fusion = pred[128,256]{1,0:T(8,128)(4,1)} fusion(s32[256]{0:T(256)S(1)} %iota_add_fusion, s32[128]{0:T(128)} %get-tuple-element.26, s32[128]{0:T(128)} %get-tuple-element.25, pred[256]{0:T(512)(128)(4,1)} %broadcast_compare_fusion.1), kind=kLoop, calls=%fused_computation.50 | loop fusion | flops 131072 | bytes 35072 | tf_op jit(solution)/shard_map/and | solution.py:110
  28.4 1.8 %pad_maximum_fusion = (bf16[256,512]{1,0:T(8,128)(2,1)S(1)}, bf16[256,512]{1,0:T(8,128)(2,1)}) fusion(bf16[128,1024]{1,0:T(8,128)(2,1)} %slice.40, bf16[128,1024]{1,0:T(8,128)(2,1)} %collective-permute-done), kind=kLoop, calls=%fused_computation.43 | loop fusion | flops 1048576 | bytes 1048576 | tf_op jit(solution)/shard_map/concatenate | solution.py:106
  30.3 0.8 copy.26
  31.1 1.6 %fusion.62 = f32[8,128]{1,0:T(8,128)S(1)} fusion(bf16[128,8,64]{0,2,1:T(8,128)(2,1)S(1)} %bitcast.62, bf16[256,8,64]{0,2,1:T(8,128)(2,1)} %bitcast.60, pred[128,256]{1,0:T(8,128)(4,1)} %and_and_fusion), kind=kOutput, calls=%fused_computation.113 | convolution fusion | flops 34865408 | bytes 430080 | tf_op jit(solution)/shard_map/sub | solution.py:40
  32.7 2.3 %fusion.7 = f32[8,128,256]{2,1,0:T(8,128)} fusion(bf16[128,8,64]{0,2,1:T(8,128)(2,1)S(1)} %bitcast.63, bf16[256,8,64]{0,2,1:T(8,128)(2,1)} %bitcast.61, pred[128,256]{1,0:T(8,128)(4,1)} %and_and_fusion), kind=kOutput, calls=%fused_computation.12 | convolution fusion | flops 34078720 | bytes 1474560 | tf_op jit(solution)/shard_map/qhd,khd->hqk/dot_general | solution.py:35
  35.1 1.8 %copy.24 = bf16[256,512]{0,1:T(8,128)(2,1)} copy(bf16[256,512]{1,0:T(8,128)(2,1)} %get-tuple-element.12) | data formatting | bytes 524288 | tf_op jit(solution)/shard_map/slice | solution.py:115
  36.9 2.0 %fusion.13 = bf16[128,8,64]{0,2,1:T(8,128)(2,1)S(1)} fusion(bf16[256,8,64]{0,2,1:T(8,128)(2,1)} %bitcast.64, f32[128,8]{0,1:T(8,128)S(1)} %bitcast.71, f32[8,128,256]{2,1,0:T(8,128)} %fusion.7, pred[128,256]{1,0:T(8,128)(4,1)} %and_and_fusion), kind=kOutput, calls=%fused_computation.22 | convolution fusion | flops 34473216 | bytes 1478656 | tf_op jit(solution)/shard_map/hqk,khd->qhd/dot_general | solution.py:42
  38.9 1.7 %fusion.8 = bf16[128,1024]{1,0:T(8,128)(2,1)S(1)} fusion(bf16[128,512]{0,1:T(8,128)(2,1)S(1)} %bitcast.65, bf16[512,1024]{1,0:T(8,128)(2,1)} %param.9, bf16[128,1024]{1,0:T(8,128)(2,1)S(1)} %copy-done.2), kind=kOutput, calls=%fused_computation.14 | convolution fusion | flops 134610944 | bytes 1703936 | tf_op jit(solution)/shard_map/dot_general | solution.py:119
  40.8 1.9 %collective-permute-start.1 = (f32[1,1024]{1,0:T(1,128)S(1)}, f32[1,1024]{1,0:T(1,128)S(1)}, u32[]{:S(2)}, u32[]{:S(2)}) collective-permute-start(f32[1,1024]{1,0:T(1,128)S(1)} %fusion.41), channel_id=1, source_target_pairs={{1,0},{2,1},{3,2},{4,3},{5,4},{6,5},{7,6},{8,7},{9,8},{10,9},{11,1... | collective-permute-start | bytes 12296 | tf_op jit(solution)/shard_map/ppermute | solution.py:20
  44.0 0.9 fusion.24
  47.1 1.4 %dynamic-update-slice = s32[16]{0:T(128)S(1)} dynamic-update-slice(s32[16]{0:T(128)S(1)} %broadcast.329, s32[1]{0:T(128)} %bitcast.12, u32[]{:T(128)} %bitcast.13) | dynamic-update-slice | bytes 12
  48.5 12.3 %all-reduce = s32[16]{0:T(128)S(1)} all-reduce(s32[16]{0:T(128)S(1)} %dynamic-update-slice), channel_id=1, replica_groups=mesh['parts'=2,'ctx'=16] {'ctx'}, use_global_device_ids=true, to_apply=%add | all-reduce | flops 16 | bytes 128
  62.4 1.3 %compare_select_fusion.1 = s32[64]{0:T(128)S(1)} fusion(s32[]{:T(128)} %get-tuple-element.19, s32[]{:T(128)} %reduce_sum.96), kind=kLoop, calls=%fused_computation.83 | loop fusion | flops 192 | bytes 264 | tf_op jit(solution)/shard_map/jit(_where)/select_n | solution.py:143
  64.1 24.3 %all-gather.2.cloned.1.call-done = bf16[1024,1024]{1,0:T(8,128)(2,1)} async-done(((bf16[64,1024]{1,0:T(8,128)(2,1)}), bf16[1024,1024]{1,0:T(8,128)(2,1)}) %all-gather.2.cloned.1.call-update) | async-done | bytes 2097168 | tf_op jit(solution)/shard_map/all_gather | solution.py:145
  88.4 3.0 %fusion.60 = (bf16[1024,512]{1,0:T(8,128)(2,1)}, bf16[1024,512]{1,0:T(8,128)(2,1)}) fusion(bf16[1024,1024]{1,0:T(8,128)(2,1)} %all-gather.2.cloned.1.call-done), kind=kLoop, calls=%fused_computation.111 | loop fusion | bytes 4194304 | tf_op jit(solution)/shard_map/slice | solution.py:57
  91.4 2.3 %copy.31 = bf16[1024,512]{0,1:T(8,128)(2,1)} copy(bf16[1024,512]{1,0:T(8,128)(2,1)} %get-tuple-element.10) | data formatting | bytes 2097152 | tf_op jit(solution)/shard_map/slice | solution.py:58
  93.7 2.3 %copy.29 = bf16[1024,512]{0,1:T(8,128)(2,1)} copy(bf16[1024,512]{1,0:T(8,128)(2,1)} %get-tuple-element.9) | data formatting | bytes 2097152 | tf_op jit(solution)/shard_map/slice | solution.py:57
  95.9 1.9 %fusion.1 = (f32[8,64]{1,0:T(8,128)S(1)}, f32[8,64,1024]{2,1,0:T(8,128)S(1)}) fusion(pred[64,1024]{1,0:T(8,128)(4,1)S(1)} %broadcast_compare_fusion, bf16[1024,8,64]{0,2,1:T(8,128)(2,1)} %bitcast.58, bf16[64,8,64]{2,1,0:T(8,128)(2,1)S(1)} %reshape.342), kind=kOutput, calls=%fused_computation.5 | convolution fusion | flops 68681216 | bytes 3278848 | tf_op jit(solution)/shard_map/qhd,khd->hqk/dot_general | solution.py:59
  98.6 0.8 fusion.12
  99.5 0.8 convert_element_type.153
  100.3 1.5 %fusion.14 = bf16[64,1024]{1,0:T(8,128)(2,1)S(1)} fusion(bf16[64,512]{1,0:T(8,128)(2,1)} %convert_element_type.153, bf16[512,1024]{1,0:T(8,128)(2,1)} %param.11, bf16[64,1024]{1,0:T(8,128)(2,1)} %copy-done.6), kind=kOutput, calls=%fused_computation.23 | convolution fusion | flops 67305472 | bytes 1376256 | tf_op jit(solution)/shard_map/dot_general | solution.py:156
  102.0 2.2 %collective-permute-start.3 = (bf16[2,1024]{1,0:T(2,128)(2,1)S(1)}, bf16[2,1024]{1,0:T(2,128)(2,1)S(1)}, u32[]{:S(2)}, u32[]{:S(2)}) collective-permute-start(bf16[2,1024]{1,0:T(2,128)(2,1)S(1)} %convolution_convert_fusion.2), channel_id=1, source_target_pairs={{0,1},{1,2},{2,3},{3,4},{4,5},{5,6},{6,7},{7,8},{8,9},{9,10},{10,1... | collective-permute-start | bytes 12296 | tf_op jit(solution)/shard_map/ppermute | solution.py:20
  104.1 3.6 %collective-permute-done.3 = bf16[2,1024]{1,0:T(2,128)(2,1)S(1)} collective-permute-done((bf16[2,1024]{1,0:T(2,128)(2,1)S(1)}, bf16[2,1024]{1,0:T(2,128)(2,1)S(1)}, u32[]{:S(2)}, u32[]{:S(2)}) %collective-permute-start.3) | collective-permute-done | bytes 4128 | tf_op jit(solution)/shard_map/ppermute | solution.py:20
  107.8 1.0 add_convert_fusion
  (58 shorter events, 11.2 us)
Async XLA Ops:
  6.5 2.0 %copy-start = (bf16[1024,1536]{1,0:T(8,128)(2,1)S(1)}, bf16[1024,1536]{1,0:T(8,128)(2,1)}, u32[]{:S(2)}) copy-start(bf16[1024,1536]{1,0:T(8,128)(2,1)} %param.8) | copy-start | bytes 9437188
  6.5 81.9 %all-gather.2.cloned.1.call-start = ((), (), s32[]{:S(2)}) async-start(), calls=%async_computation | async-start | bytes 2228224 | tf_op jit(solution)/shard_map/all_gather | solution.py:145
  8.5 4.2 %copy-start.7 = (s32[128]{0:T(128)S(1)}, s32[128]{0:T(128)}, u32[]{:S(2)}) copy-start(s32[128]{0:T(128)} %param.7) | copy-start | bytes 1540
  10.8 17.6 %collective-permute-start = (bf16[128,1024]{1,0:T(8,128)(2,1)}, bf16[128,1024]{1,0:T(8,128)(2,1)}, u32[]{:S(2)}, u32[]{:S(2)}) collective-permute-start(bf16[128,1024]{1,0:T(8,128)(2,1)} %slice.40), channel_id=1, source_target_pairs={{0,1},{1,2},{2,3},{3,4},{4,5},{5,6},{6,7},{7,8},{8,9},{9,10},{10,1... | collective-permute-start | bytes 786440 | tf_op jit(solution)/shard_map/ppermute | solution.py:20
  16.6 26.1 %collective-permute-start.2 = (f32[1]{0:T(128)}, f32[1]{0:T(128)}, u32[]{:S(2)}, u32[]{:S(2)}) collective-permute-start(f32[1]{0:T(128)} %bitcast.10), channel_id=1, source_target_pairs={{1,0},{2,1},{3,2},{4,3},{5,4},{6,5},{7,6},{8,7},{9,8},{10,9},{11,1... | collective-permute-start | bytes 20 | tf_op jit(solution)/shard_map/ppermute | solution.py:20
  32.7 6.2 %copy-start.2 = (bf16[128,1024]{1,0:T(8,128)(2,1)S(1)}, bf16[128,1024]{1,0:T(8,128)(2,1)}, u32[]{:S(2)}) copy-start(bf16[128,1024]{1,0:T(8,128)(2,1)} %param.6) | copy-start | bytes 786436
  38.9 6.1 %copy-start.1 = (bf16[1024,1536]{1,0:T(8,128)(2,1)S(1)}, bf16[1024,1536]{1,0:T(8,128)(2,1)}, u32[]{:S(2)}) copy-start(bf16[1024,1536]{1,0:T(8,128)(2,1)} %param.10) | copy-start | bytes 9437188
  40.6 3.4 %copy-start.4 = (bf16[128,1024]{1,0:T(8,128)(2,1)}, bf16[128,1024]{1,0:T(8,128)(2,1)S(1)}, u32[]{:S(2)}) copy-start(bf16[128,1024]{1,0:T(8,128)(2,1)S(1)} %fusion.8) | copy-start | bytes 786436
  40.8 3.2 %collective-permute-start.1 = (f32[1,1024]{1,0:T(1,128)S(1)}, f32[1,1024]{1,0:T(1,128)S(1)}, u32[]{:S(2)}, u32[]{:S(2)}) collective-permute-start(f32[1,1024]{1,0:T(1,128)S(1)} %fusion.41), channel_id=1, source_target_pairs={{1,0},{2,1},{3,2},{4,3},{5,4},{6,5},{7,6},{8,7},{9,8},{10,9},{11,1... | collective-permute-start | bytes 12296 | tf_op jit(solution)/shard_map/ppermute | solution.py:20
  44.9 0.8 copy-start.6
  44.9 1.5 %copy-start.8 = (u32[32]{0:T(128)S(1)}, u32[32]{0:T(128)}, u32[]{:S(2)}) copy-start(u32[32]{0:T(128)} %constant.78) | copy-start | bytes 388
  95.9 2.6 %copy-start.3 = (bf16[1024,512]{0,1:T(8,128)(2,1)S(1)}, bf16[1024,512]{0,1:T(8,128)(2,1)}, u32[]{:S(2)}) copy-start(bf16[1024,512]{0,1:T(8,128)(2,1)} %copy.31) | copy-start | bytes 3145732
  98.6 9.2 %copy-start.5 = (bf16[128,1024]{1,0:T(8,128)(2,1)S(1)}, bf16[128,1024]{1,0:T(8,128)(2,1)}, u32[]{:S(2)}) copy-start(bf16[128,1024]{1,0:T(8,128)(2,1)} %copy-done.4) | copy-start | bytes 786436
  102.0 5.8 %collective-permute-start.3 = (bf16[2,1024]{1,0:T(2,128)(2,1)S(1)}, bf16[2,1024]{1,0:T(2,128)(2,1)S(1)}, u32[]{:S(2)}, u32[]{:S(2)}) collective-permute-start(bf16[2,1024]{1,0:T(2,128)(2,1)S(1)} %convolution_convert_fusion.2), channel_id=1, source_target_pairs={{0,1},{1,2},{2,3},{3,4},{4,5},{5,6},{6,7},{7,8},{8,9},{9,10},{10,1... | collective-permute-start | bytes 12296 | tf_op jit(solution)/shard_map/ppermute | solution.py:20
Sparse Core Ops, SparseCore 0:
  46.5 41.8 all-gather.1
where the time goes:
time: 116 us
  waiting for transfers between devices  28.7 us (25%)
  local copies, waits for them, and re-layouts  17.9 us (15%)
  matrix products  16.4 us (14%)
  between operations  15.1 us (13%)
  other arithmetic  14.7 us (13%)
  blocking collectives  12.3 us (11%)
  starting transfers between devices  10.5 us (9%)
    all_gather x1, waiting for transfers between devices, shards(): lax.all_gather(ragged_packed[:, inner_width:], 'ctx', axis=0, tiled=True)  24.3 us
    unnamed x1, blocking collectives  12.3 us
    ppermute x4, starting transfers between devices, from_behind(): return lax.ppermute(block, axis, route)  10.5 us
    slice x2, local copies, waits for them, and re-layouts, absorb(): key_slice[:, :inner_width].reshape(block_end - block_start, HEADS, HEAD_DIM)  5.25 us
    ppermute x4, waiting for transfers between devices, from_behind(): return lax.ppermute(block, axis, route)  4.36 us
    unnamed x21, local copies, waits for them, and re-layouts  2.84 us
    dot_general x1, matrix products, window_attend(): jnp.einsum('qhd,khd->hqk', query_heads, key_heads, preferred_element_type...  2.33 us
  transfers between devices with their start and end apart: 5, of which 3 were waited for; matrix products, arithmetic and copies ran while one was open for 24% of the time, Pallas kernels for 0%

commit v1 on v0

v1 whole, which is shorter than its diff:
```python
import functools

import jax
import jax.numpy as jnp
from jax import lax
from jax.experimental import pallas as pl
from jax.experimental.pallas import tpu as pltpu
from jax.sharding import PartitionSpec as P

HEADS = 8
HEAD_DIM = 64
WINDOW = 128
INNER = HEADS * HEAD_DIM
PAIR = 2 * HEAD_DIM
GROUP = 4
TAIL = 16
EPSILON = 1e-06
MASKED = -1e30
SCALE = HEAD_DIM ** (-0.5)
F32 = jnp.float32
BF16 = jnp.bfloat16
NT = (((1,), (1,)), ((), ()))


def normalize(matrix):
    values = matrix.astype(F32)
    inverse = lax.rsqrt(jnp.mean(values * values, axis=-1, keepdims=True) + EPSILON)
    return (values * inverse).astype(BF16)


def dot(a, b):
    return jnp.dot(a, b, preferred_element_type=F32)


def iota(shape, dim):
    return lax.broadcasted_iota(jnp.int32, shape, dim)


def onehot(condition):
    return jnp.where(condition, 1.0, 0.0).astype(BF16)


def stack_heads(q_pair):
    low = iota(q_pair.shape, 1) < HEAD_DIM
    zero = jnp.zeros_like(q_pair)
    return jnp.concatenate([jnp.where(low, q_pair, zero), jnp.where(low, zero, q_pair)], axis=0)


def unstack_heads(stacked):
    rows = stacked.shape[0] // 2
    low = iota((rows, PAIR), 1) < HEAD_DIM
    return jnp.where(low, stacked[:rows], stacked[rows:])


def kernel(
    n, tokens, boundary, wqf_hbm, wof_hbm, wqs_hbm, wos_hbm, out,
    wqf, wof, wqs, wos, prev, kv_cat, lead_out, lead_in, marks, parted, joined, rows_out, rows_in,
    kv_all, mix, mix_tail,
    w_sem, tok_s, tok_r, lead_s, lead_r, marks_s, marks_r, part_s, part_r, rows_s, rows_r,
    kv_s, kv_r, mix_s, mix_r, mt_s, mt_r,
):
    length, width = tokens.shape
    capacity = length // 2
    groups = n // GROUP
    me = lax.axis_index("ctx")
    group = me // GROUP
    lane = lax.rem(me, GROUP)

    def remote(src, dst, s_sem, r_sem, device):
        return pltpu.make_async_remote_copy(
            src_ref=src, dst_ref=dst, send_sem=s_sem, recv_sem=r_sem,
            device_id={"ctx": device}, device_id_type=pl.DeviceIdType.MESH,
        )

    weights = [
        pltpu.make_async_copy(src, dst, w_sem.at[i])
        for i, (src, dst) in enumerate([(wqf_hbm, wqf), (wof_hbm, wof), (wqs_hbm, wqs), (wos_hbm, wos)])
    ]

    barrier = pltpu.get_barrier_semaphore()

    def greet(k, carry):
        pl.semaphore_signal(
            barrier, inc=1, device_id={"ctx": lax.rem(me + k, n)}, device_id_type=pl.DeviceIdType.MESH
        )
        return carry

    lax.fori_loop(1, n, greet, 0)
    for copy in weights:
        copy.start()

    after = lax.rem(me + 1, n)
    before = lax.rem(me + n - 1, n)
    peers = [lax.rem(lane + k, GROUP) for k in range(1, GROUP)]
    bound = boundary[...]
    marks[lane] = jnp.broadcast_to(bound, (8, length))

    @pl.when(me == 0)
    def _():
        prev[...] = jnp.zeros_like(prev)
        rows_in[...] = jnp.zeros_like(rows_in)

    @pl.when(me == n - 1)
    def _():
        lead_in[...] = jnp.zeros_like(lead_in)

    @pl.when((lane != 0) | (group == 0))
    def _():
        mix_tail[...] = jnp.zeros_like(mix_tail)

    pl.semaphore_wait(barrier, n - 1)

    tok_copy = remote(tokens, prev, tok_s, tok_r, after)

    @pl.when(me < n - 1)
    def _():
        tok_copy.start()

    marks_copies = [
        remote(marks.at[lane], marks.at[lane], marks_s.at[k], marks_r.at[lane], group * GROUP + peer)
        for k, peer in enumerate(peers)
    ]
    for copy in marks_copies:
        copy.start()

    tok = tokens[...]
    normed = normalize(tok)
    weights[0].wait()
    packed = dot(normed, wqf[...]).astype(BF16)
    queries = packed[:, :INNER]
    kv_cat[length:, :] = packed[:, INNER:]

    bound_rows = jnp.broadcast_to(bound.astype(F32), (length, length)).astype(BF16)
    i0 = iota((length, length), 0)
    i1 = iota((length, length), 1)
    seg_lane = dot(bound_rows, onehot(i0 <= i1)).astype(jnp.int32) - 1
    seg_sub = lax.dot_general(onehot(i1 <= i0), bound_rows, NT, preferred_element_type=F32).astype(jnp.int32) - 1
    starts = jnp.sum(bound, axis=1, keepdims=True)

    @pl.when(me > 0)
    def _():
        remote(tokens, prev, tok_s, tok_r, before).wait_recv()

    kv_cat[:length, :] = dot(normalize(prev[...]), wqf[:, INNER:]).astype(BF16)

    q_pos = iota((length, 2 * length), 0) + length
    k_pos = iota((length, 2 * length), 1)
    first_key = jnp.where(me == 0, length, 0)
    allowed = (k_pos <= q_pos) & (k_pos > q_pos - WINDOW) & (k_pos >= first_key)
    allowed = jnp.concatenate([allowed, allowed], axis=0)
    mixed = []
    for p in range(HEADS // 2):
        cols = slice(p * PAIR, (p + 1) * PAIR)
        scores = lax.dot_general(stack_heads(queries[:, cols]), kv_cat[:, cols], NT, preferred_element_type=F32)
        scores = jnp.where(allowed, scores, MASKED)
        highest = jnp.max(scores, axis=-1, keepdims=True)
        expsum = jnp.exp((scores - highest) * SCALE)
        total = jnp.sum(expsum, axis=-1, keepdims=True)
        values = kv_cat[:, INNER + p * PAIR:INNER + (p + 1) * PAIR]
        mixed.append(unstack_heads(dot(expsum.astype(BF16), values) / total).astype(BF16))
    weights[1].wait()
    stream = (tok.astype(F32) + dot(jnp.concatenate(mixed, axis=1), wof[...])).astype(BF16)

    slots = capacity + TAIL
    slot = iota((slots, length), 0)
    gather = onehot(jnp.where(slot == capacity, -1, slot) == seg_lane[:slots])
    partial = dot(gather, stream)
    sizes = jnp.sum(gather.astype(F32), axis=1, keepdims=True)
    lead_out[:, :width] = partial[capacity:capacity + 8]
    lead_out[:, width:] = jnp.broadcast_to(sizes[capacity:capacity + 8], (8, 128))
    lead_copy = remote(lead_out, lead_in, lead_s, lead_r, before)

    @pl.when(me > 0)
    def _():
        lead_copy.start()

    slot_col = iota((capacity, 1), 0)
    closing = jnp.where(slot_col == starts - 1, 1.0, 0.0)
    weights[2].wait()

    @pl.when(me < n - 1)
    def _():
        remote(lead_out, lead_in, lead_s, lead_r, after).wait_recv()

    lead = lead_in[0:1, :]
    totals = partial[:capacity] + closing * lead[:, :width]
    seg_sizes = sizes[:capacity] + closing * lead[:, width:width + 1]
    pooled = (totals / jnp.maximum(seg_sizes, 1.0)).astype(BF16)

    short = dot(normalize(pooled), wqs[...]).astype(BF16)
    for j in range(GROUP):
        for part in range(3):
            parted[j, :, part * PAIR:(part + 1) * PAIR] = short[:, part * INNER + j * PAIR:part * INNER + (j + 1) * PAIR]
    part_copies = [
        remote(parted.at[peer], joined.at[lane], part_s.at[k], part_r.at[lane], group * GROUP + peer)
        for k, peer in enumerate(peers)
    ]
    for copy in part_copies:
        copy.start()
    joined[lane] = parted[lane]

    tail_row = iota((TAIL, capacity), 0)
    tail_slot = iota((TAIL, capacity), 1)
    rows_out[...] = dot(onehot((tail_row < 2) & (tail_slot == starts - 1 - tail_row)), pooled).astype(BF16)
    rows_copy = remote(rows_out, rows_in, rows_s, rows_r, after)

    @pl.when(me < n - 1)
    def _():
        rows_copy.start()

    for k, peer in enumerate(peers):
        remote(marks.at[lane], marks.at[peer], marks_s.at[k], marks_r.at[peer], group * GROUP + peer).wait_recv()
    counts = [jnp.sum(marks[j][0:1], axis=1, keepdims=True) for j in range(GROUP)]
    firsts = [jnp.zeros_like(counts[0])]
    for j in range(GROUP - 1):
        firsts.append(firsts[-1] + counts[j])
    my_first = firsts[0]
    for j in range(1, GROUP):
        my_first = jnp.where(lane == j, firsts[j], my_first)

    place = iota((length, GROUP * capacity), 0)
    source = iota((length, GROUP * capacity), 1)
    owner_first = jnp.broadcast_to(firsts[0], place.shape)
    owner_count = jnp.broadcast_to(counts[0], place.shape)
    for j in range(1, GROUP):
        beyond = source >= j * capacity
        owner_first = jnp.where(beyond, firsts[j], owner_first)
        owner_count = jnp.where(beyond, counts[j], owner_count)
    within = source & (capacity - 1)
    compact = onehot((within < owner_count) & (within + owner_first == place))

    for k, peer in enumerate(peers):
        remote(parted.at[lane], joined.at[peer], part_s.at[k], part_r.at[peer], group * GROUP + peer).wait_recv()
    rows = dot(compact, joined[...].reshape(GROUP * capacity, 3 * PAIR)).astype(BF16)
    kv_all[group] = rows[:, PAIR:]

    def kv_copy(other):
        return remote(kv_all.at[group], kv_all.at[group], kv_s.at[other], kv_r.at[group], other * GROUP + lane)

    def send(other, carry):
        kv_copy(other).start()
        return carry

    lax.fori_loop(group + 1, groups, send, 0)

    q_stack = stack_heads(rows[:, :PAIR])
    scores = lax.dot_general(q_stack, rows[:, PAIR:2 * PAIR], NT, preferred_element_type=F32)
    causal = i1 <= i0
    scores = jnp.where(jnp.concatenate([causal, causal], axis=0), scores, MASKED)
    row_max = jnp.max(scores, axis=-1, keepdims=True)
    expsum = jnp.exp((scores - row_max) * SCALE)
    row_total = jnp.sum(expsum, axis=-1, keepdims=True)
    running = dot(expsum.astype(BF16), rows[:, 2 * PAIR:])

    @pl.when(me > 0)
    def _():
        remote(rows_out, rows_in, rows_s, rows_r, before).wait_recv()

    lift = onehot(iota((length, capacity), 1) == seg_sub[:, :capacity] - 1)
    lift_tail = onehot(iota((length, TAIL), 1) == -seg_sub[:, :TAIL])
    pooled_lifted = dot(lift, pooled) + dot(lift_tail, rows_in[...])

    def attend(step, carry):
        row_max, row_total, running = carry
        other = group - 1 - step
        remote(
            kv_all.at[other], kv_all.at[other], kv_s.at[other], kv_r.at[other], other * GROUP + lane
        ).wait_recv()
        block = kv_all[other]
        scores = lax.dot_general(q_stack, block[:, :PAIR], NT, preferred_element_type=F32)
        new_max = jnp.maximum(row_max, jnp.max(scores, axis=-1, keepdims=True))
        expsum = jnp.exp((scores - new_max) * SCALE)
        fading = jnp.exp((row_max - new_max) * SCALE)
        row_total = row_total * fading + jnp.sum(expsum, axis=-1, keepdims=True)
        running = running * fading + dot(expsum.astype(BF16), block[:, PAIR:])
        return new_max, row_total, running

    row_max, row_total, running = lax.fori_loop(0, group, attend, (row_max, row_total, running))
    mix[lane] = unstack_heads(running / row_total).astype(BF16)

    mix_copies = [
        remote(mix.at[lane], mix.at[lane], mix_s.at[k], mix_r.at[lane], group * GROUP + peer)
        for k, peer in enumerate(peers)
    ]
    for copy in mix_copies:
        copy.start()
    next_lead = lax.rem((group + 1) * GROUP, n)
    mt_copy = remote(
        mix.at[lane, pl.ds(length - TAIL, TAIL)], mix_tail.at[lane], mt_s, mt_r.at[lane], next_lead
    )

    @pl.when(group < groups - 1)
    def _():
        mt_copy.start()

    weights[3].wait()
    target = seg_sub + my_first - 1
    pick = onehot(i1 == target)
    pick_tail = onehot(iota((length, TAIL), 1) == target[:, :TAIL] + TAIL)
    for k, peer in enumerate(peers):
        remote(mix.at[peer], mix.at[peer], mix_s.at[k], mix_r.at[peer], group * GROUP + peer).wait_recv()

    @pl.when((lane == 0) & (group > 0))
    def _():
        for j in range(GROUP):
            remote(
                mix.at[j, pl.ds(length - TAIL, TAIL)], mix_tail.at[j], mt_s, mt_r.at[j], before
            ).wait_recv()

    mixed_rows = jnp.concatenate([mix[j] for j in range(GROUP)], axis=1)
    tail_rows = jnp.concatenate([mix_tail[j] for j in range(GROUP)], axis=1)
    lifted = (dot(pick, mixed_rows) + dot(pick_tail, tail_rows)).astype(BF16)
    short_out = (pooled_lifted + dot(lifted, wos[...])).astype(BF16)
    out[...] = (stream.astype(F32) + short_out.astype(F32)).astype(BF16)

    @pl.when(me < n - 1)
    def _():
        tok_copy.wait_send()
        rows_copy.wait_send()

    @pl.when(me > 0)
    def _():
        lead_copy.wait_send()

    for copy in marks_copies + part_copies + mix_copies:
        copy.wait_send()

    def drain(other, carry):
        kv_copy(other).wait_send()
        return carry

    lax.fori_loop(group + 1, groups, drain, 0)

    @pl.when(group < groups - 1)
    def _():
        mt_copy.wait_send()


def shards(n, tokens, boundary, w_qkv_full, w_out_full, w_qkv_short, w_out_short):
    length, width = tokens.shape
    capacity = length // 2
    groups = n // GROUP
    vmem = pl.BlockSpec(memory_space=pltpu.VMEM)
    hbm = pl.BlockSpec(memory_space=pl.ANY)
    dma = pltpu.SemaphoreType.DMA
    return pl.pallas_call(
        functools.partial(kernel, n),
        out_shape=jax.ShapeDtypeStruct((length, width), BF16),
        in_specs=[vmem, vmem, hbm, hbm, hbm, hbm],
        out_specs=vmem,
        scratch_shapes=[
            pltpu.VMEM(w_qkv_full.shape, BF16),
            pltpu.VMEM(w_out_full.shape, BF16),
            pltpu.VMEM(w_qkv_short.shape, BF16),
            pltpu.VMEM(w_out_short.shape, BF16),
            pltpu.VMEM((length, width), BF16),
            pltpu.VMEM((2 * length, 2 * INNER), BF16),
            pltpu.VMEM((8, width + 128), F32),
            pltpu.VMEM((8, width + 128), F32),
            pltpu.VMEM((GROUP, 8, length), jnp.int32),
            pltpu.VMEM((GROUP, capacity, 3 * PAIR), BF16),
            pltpu.VMEM((GROUP, capacity, 3 * PAIR), BF16),
            pltpu.VMEM((TAIL, width), BF16),
            pltpu.VMEM((TAIL, width), BF16),
            pltpu.VMEM((groups, length, 2 * PAIR), BF16),
            pltpu.VMEM((GROUP, length, PAIR), BF16),
            pltpu.VMEM((GROUP, TAIL, PAIR), BF16),
            dma((4,)),
            dma, dma, dma, dma,
            dma((GROUP,)), dma((GROUP,)),
            dma((GROUP,)), dma((GROUP,)),
            dma, dma,
            dma((groups,)), dma((groups,)),
            dma((GROUP,)), dma((GROUP,)),
            dma, dma((GROUP,)),
        ],
        compiler_params=pltpu.CompilerParams(
            collective_id=0, has_side_effects=True, vmem_limit_bytes=40 * 1024 * 1024
        ),
    )(tokens, boundary.reshape(1, length), w_qkv_full, w_out_full, w_qkv_short, w_out_short)


def solution(mesh):
    return jax.shard_map(
        functools.partial(shards, mesh.shape["ctx"]),
        mesh=mesh,
        in_specs=(P(("parts", "ctx"), None), P(("parts", "ctx")), P(), P(), P(), P()),
        out_specs=P(("parts", "ctx"), None),
        check_vma=False,
    )
```

time: 116 us -> 37.3 us (0.32)
  the two profiles are of different devices: /device:TPU:8 before, /device:TPU:25 now
where the time goes in v1:
time: 37.3 us; the launch traced here: 36.9 us
  Pallas kernels  28.3 us (76%)
  local copies, waits for them, and re-layouts  8.54 us (23%)
    pallas_call x1, Pallas kernels, shards(): pl.pallas_call(functools.partial(kernel, n), out_shape=jax.ShapeDtypeStru...  28.3 us
    unnamed x13, local copies, waits for them, and re-layouts  8.54 us

profile of v1, /device:TPU:25, one launch (start us, length us, event | category | flops | bytes accessed | tf_op | source)
XLA Modules:
  0.0 36.9 jit_solution(2240842474098496855)
XLA Ops:
  0.0 0.0 copy-start
  0.0 1.9 %copy-done = bf16[1024,1536]{1,0:T(8,128)(2,1)S(1)} copy-done((bf16[1024,1536]{1,0:T(8,128)(2,1)S(1)}, bf16[1024,1536]{1,0:T(8,128)(2,1)}, u32[]{:S(2)}) %copy-start) | copy-done | bytes 3145752
  1.9 0.0 copy-start.1
  1.9 1.9 %copy-done.1 = bf16[1024,1536]{1,0:T(8,128)(2,1)S(1)} copy-done((bf16[1024,1536]{1,0:T(8,128)(2,1)S(1)}, bf16[1024,1536]{1,0:T(8,128)(2,1)}, u32[]{:S(2)}) %copy-start.1) | copy-done | bytes 3145752
  3.8 0.0 copy-start.2
  3.8 1.2 %copy-done.2 = bf16[512,1024]{1,0:T(8,128)(2,1)S(1)} copy-done((bf16[512,1024]{1,0:T(8,128)(2,1)S(1)}, bf16[512,1024]{1,0:T(8,128)(2,1)}, u32[]{:S(2)}) %copy-start.2) | copy-done | bytes 1048600
  5.0 0.0 copy-start.3
  5.0 1.2 %copy-done.3 = bf16[512,1024]{1,0:T(8,128)(2,1)S(1)} copy-done((bf16[512,1024]{1,0:T(8,128)(2,1)S(1)}, bf16[512,1024]{1,0:T(8,128)(2,1)}, u32[]{:S(2)}) %copy-start.3) | copy-done | bytes 1048600
  6.2 0.0 copy-start.4
  6.2 0.9 %copy-done.4 = bf16[128,1024]{1,0:T(8,128)(2,1)S(1)} copy-done((bf16[128,1024]{1,0:T(8,128)(2,1)S(1)}, bf16[128,1024]{1,0:T(8,128)(2,1)}, u32[]{:S(2)}) %copy-start.4) | copy-done | bytes 262168
  7.2 0.0 copy-start.5
  7.2 0.7 %copy-done.5 = s32[128]{0:T(128)S(1)} copy-done((s32[128]{0:T(128)S(1)}, s32[128]{0:T(128)}, u32[]{:S(2)}) %copy-start.5) | copy-done | bytes 536
  7.8 28.3 %shard_map.64 = bf16[128,1024]{1,0:T(8,128)(2,1)S(1)} custom-call(bf16[128,1024]{1,0:T(8,128)(2,1)S(1)} %copy-done.4, s32[1,128]{1,0:T(1,128)S(1)} %bitcast.1, bf16[1024,1536]{1,0:T(8,128)(2,1)S(1)} %copy-done, bf16[512,1024]{1,0:T(8,128)(2,1)S(1)} %copy-done.2, bf16[1024,1536]{1,0:T(8,128)(2,1)S(1)} %copy-done.1, bf16[512,1024]{1,0:T(8,128)(2,1)S(1)} %copy-done.3), custom_call_target="tpu_custom_call" | custom-call | tf_op jit(solution)/shard_map/pallas_call | solution.py:346
  36.1 0.7 %copy.8 = bf16[128,1024]{1,0:T(8,128)(2,1)} copy(bf16[128,1024]{1,0:T(8,128)(2,1)S(1)} %shard_map.64) | data formatting | bytes 524288
Async XLA Ops:
  0.0 1.9 %copy-start = (bf16[1024,1536]{1,0:T(8,128)(2,1)S(1)}, bf16[1024,1536]{1,0:T(8,128)(2,1)}, u32[]{:S(2)}) copy-start(bf16[1024,1536]{1,0:T(8,128)(2,1)} %wqf_hbm.1) | copy-start | bytes 9437188
  1.9 1.9 %copy-start.1 = (bf16[1024,1536]{1,0:T(8,128)(2,1)S(1)}, bf16[1024,1536]{1,0:T(8,128)(2,1)}, u32[]{:S(2)}) copy-start(bf16[1024,1536]{1,0:T(8,128)(2,1)} %wqs_hbm.1) | copy-start | bytes 9437188
  3.8 1.2 %copy-start.2 = (bf16[512,1024]{1,0:T(8,128)(2,1)S(1)}, bf16[512,1024]{1,0:T(8,128)(2,1)}, u32[]{:S(2)}) copy-start(bf16[512,1024]{1,0:T(8,128)(2,1)} %wof_hbm.1) | copy-start | bytes 3145732
  5.0 1.2 %copy-start.3 = (bf16[512,1024]{1,0:T(8,128)(2,1)S(1)}, bf16[512,1024]{1,0:T(8,128)(2,1)}, u32[]{:S(2)}) copy-start(bf16[512,1024]{1,0:T(8,128)(2,1)} %wos_hbm.1) | copy-start | bytes 3145732
  6.2 0.9 %copy-start.4 = (bf16[128,1024]{1,0:T(8,128)(2,1)S(1)}, bf16[128,1024]{1,0:T(8,128)(2,1)}, u32[]{:S(2)}) copy-start(bf16[128,1024]{1,0:T(8,128)(2,1)} %tokens.1) | copy-start | bytes 786436
  7.2 0.7 %copy-start.5 = (s32[128]{0:T(128)S(1)}, s32[128]{0:T(128)}, u32[]{:S(2)}) copy-start(s32[128]{0:T(128)} %param.7) | copy-start | bytes 1540

commit v2 on v1

--- a/solution.py
+++ b/solution.py
@@ -53,8 +53,8 @@
 
 
 def kernel(
-    n, tokens, boundary, wqf_hbm, wof_hbm, wqs_hbm, wos_hbm, out,
-    wqf, wof, wqs, wos, prev, kv_cat, lead_out, lead_in, marks, parted, joined, rows_out, rows_in,
+    n, tokens_hbm, boundary_hbm, wqf_hbm, wof_hbm, wqs_hbm, wos_hbm, out,
+    tokens, boundary, wqf, wof, wqs, wos, prev, kv_cat, lead_out, lead_in, marks, parted, joined, rows_out, rows_in,
     kv_all, mix, mix_tail,
     w_sem, tok_s, tok_r, lead_s, lead_r, marks_s, marks_r, part_s, part_r, rows_s, rows_r,
     kv_s, kv_r, mix_s, mix_r, mt_s, mt_r,
@@ -74,7 +74,10 @@
 
     weights = [
         pltpu.make_async_copy(src, dst, w_sem.at[i])
-        for i, (src, dst) in enumerate([(wqf_hbm, wqf), (wof_hbm, wof), (wqs_hbm, wqs), (wos_hbm, wos)])
+        for i, (src, dst) in enumerate([
+            (wqf_hbm, wqf), (wof_hbm, wof), (wqs_hbm, wqs), (wos_hbm, wos),
+            (tokens_hbm, tokens), (boundary_hbm, boundary),
+        ])
     ]
 
     barrier = pltpu.get_barrier_semaphore()
@@ -86,12 +89,13 @@
         return carry
 
     lax.fori_loop(1, n, greet, 0)
-    for copy in weights:
-        copy.start()
+    for i in (4, 5, 0, 1, 2, 3):
+        weights[i].start()
 
     after = lax.rem(me + 1, n)
     before = lax.rem(me + n - 1, n)
     peers = [lax.rem(lane + k, GROUP) for k in range(1, GROUP)]
+    weights[5].wait()
     bound = boundary[...]
     marks[lane] = jnp.broadcast_to(bound, (8, length))
 
@@ -108,9 +112,19 @@
     def _():
         mix_tail[...] = jnp.zeros_like(mix_tail)
 
+    bound_rows = jnp.broadcast_to(bound.astype(F32), (length, length)).astype(BF16)
+    i0 = iota((length, length), 0)
+    i1 = iota((length, length), 1)
+    seg_lane = dot(bound_rows, onehot(i0 <= i1)).astype(jnp.int32) - 1
+    seg_sub = lax.dot_general(onehot(i1 <= i0), bound_rows, NT, preferred_element_type=F32).astype(jnp.int32) - 1
+    starts = jnp.sum(bound, axis=1, keepdims=True)
+
+    weights[4].wait()
+    tok = tokens[...]
+    normed = normalize(tok)
     pl.semaphore_wait(barrier, n - 1)
 
-    tok_copy = remote(tokens, prev, tok_s, tok_r, after)
+    tok_copy = remote(tokens_hbm, prev, tok_s, tok_r, after)
 
     @pl.when(me < n - 1)
     def _():
@@ -123,23 +137,14 @@
     for copy in marks_copies:
         copy.start()
 
-    tok = tokens[...]
-    normed = normalize(tok)
     weights[0].wait()
     packed = dot(normed, wqf[...]).astype(BF16)
     queries = packed[:, :INNER]
     kv_cat[length:, :] = packed[:, INNER:]
 
-    bound_rows = jnp.broadcast_to(bound.astype(F32), (length, length)).astype(BF16)
-    i0 = iota((length, length), 0)
-    i1 = iota((length, length), 1)
-    seg_lane = dot(bound_rows, onehot(i0 <= i1)).astype(jnp.int32) - 1
-    seg_sub = lax.dot_general(onehot(i1 <= i0), bound_rows, NT, preferred_element_type=F32).astype(jnp.int32) - 1
-    starts = jnp.sum(bound, axis=1, keepdims=True)
-
     @pl.when(me > 0)
     def _():
-        remote(tokens, prev, tok_s, tok_r, before).wait_recv()
+        remote(tokens_hbm, prev, tok_s, tok_r, before).wait_recv()
 
     kv_cat[:length, :] = dot(normalize(prev[...]), wqf[:, INNER:]).astype(BF16)
 
@@ -346,9 +351,11 @@
     return pl.pallas_call(
         functools.partial(kernel, n),
         out_shape=jax.ShapeDtypeStruct((length, width), BF16),
-        in_specs=[vmem, vmem, hbm, hbm, hbm, hbm],
+        in_specs=[hbm, hbm, hbm, hbm, hbm, hbm],
         out_specs=vmem,
         scratch_shapes=[
+            pltpu.VMEM((length, width), BF16),
+            pltpu.VMEM((1, length), jnp.int32),
             pltpu.VMEM(w_qkv_full.shape, BF16),
             pltpu.VMEM(w_out_full.shape, BF16),
             pltpu.VMEM(w_qkv_short.shape, BF16),
@@ -365,7 +372,7 @@
             pltpu.VMEM((groups, length, 2 * PAIR), BF16),
             pltpu.VMEM((GROUP, length, PAIR), BF16),
             pltpu.VMEM((GROUP, TAIL, PAIR), BF16),
-            dma((4,)),
+            dma((6,)),
             dma, dma, dma, dma,
             dma((GROUP,)), dma((GROUP,)),
             dma((GROUP,)), dma((GROUP,)),
@@ -375,7 +382,7 @@
             dma, dma((GROUP,)),
         ],
         compiler_params=pltpu.CompilerParams(
-            collective_id=0, has_side_effects=True, vmem_limit_bytes=40 * 1024 * 1024
+            collective_id=0, has_side_effects=True, vmem_limit_bytes=60 * 1024 * 1024
         ),
     )(tokens, boundary.reshape(1, length), w_qkv_full, w_out_full, w_qkv_short, w_out_short)
 

time: 37.3 us -> 31.1 us (0.83)
  local copies, waits for them, and re-layouts: 8.54 us -> 1.67 us
  Pallas kernels: 28.3 us -> 29.2 us
    unnamed x13 -> x1, local copies, waits for them, and re-layouts: 8.54 us -> 1.67 us
    pallas_call x1, Pallas kernels: 28.3 us -> 29.2 us  [shards(): pl.pallas_call(functools.partial(kernel, n), out_shape=jax.ShapeDtypeStru...]
where the time goes in v2:
time: 31.1 us; the launch traced here: 30.9 us
  Pallas kernels  29.2 us (94%)
  local copies, waits for them, and re-layouts  1.67 us (5%)
    pallas_call x1, Pallas kernels, shards(): pl.pallas_call(functools.partial(kernel, n), out_shape=jax.ShapeDtypeStru...  29.2 us
    unnamed x1, local copies, waits for them, and re-layouts  1.67 us

profile of v2, /device:TPU:25, one launch (start us, length us, event | category | flops | bytes accessed | tf_op | source)
XLA Modules:
  0.0 30.9 jit_solution(2160472344184344357)
XLA Ops:
  0.0 29.2 %shard_map.64 = bf16[128,1024]{1,0:T(8,128)(2,1)} custom-call(bf16[128,1024]{1,0:T(8,128)(2,1)} %tokens_hbm.1, s32[1,128]{1,0:T(1,128)} %bitcast.1, bf16[1024,1536]{1,0:T(8,128)(2,1)} %wqf_hbm.1, bf16[512,1024]{1,0:T(8,128)(2,1)} %wof_hbm.1, bf16[1024,1536]{1,0:T(8,128)(2,1)} %wqs_hbm.1, bf16[512,1024]{1,0:T(8,128)(2,1)} %wos_hbm.1), custom_call_target="tpu_custom_call" | custom-call | tf_op jit(solution)/shard_map/pallas_call | solution.py:351
  29.2 1.7 %copy.8 = bf16[128,1024]{1,0:T(8,128)(2,1)} copy(bf16[128,1024]{1,0:T(8,128)(2,1)} %shard_map.64) | data formatting | bytes 524288

commit v3 on v2

--- a/solution.py
+++ b/solution.py
@@ -54,9 +54,9 @@
 
 def kernel(
     n, tokens_hbm, boundary_hbm, wqf_hbm, wof_hbm, wqs_hbm, wos_hbm, out,
-    tokens, boundary, wqf, wof, wqs, wos, prev, kv_cat, lead_out, lead_in, marks, parted, joined, rows_out, rows_in,
+    tokens, boundary, wqf, wof, wqs, wos, prev, kv_cat, edges, marks, parted, joined,
     kv_all, mix, mix_tail,
-    w_sem, tok_s, tok_r, lead_s, lead_r, marks_s, marks_r, part_s, part_r, rows_s, rows_r,
+    w_sem, tok_s, tok_r, edge_s, edge_r, marks_s, marks_r, part_s, part_r,
     kv_s, kv_r, mix_s, mix_r, mt_s, mt_r,
 ):
     length, width = tokens.shape
@@ -102,11 +102,14 @@
     @pl.when(me == 0)
     def _():
         prev[...] = jnp.zeros_like(prev)
-        rows_in[...] = jnp.zeros_like(rows_in)
-
-    @pl.when(me == n - 1)
-    def _():
-        lead_in[...] = jnp.zeros_like(lead_in)
+
+    @pl.when(group == groups - 1)
+    def _():
+        edges[GROUP] = jnp.zeros(edges.shape[1:], F32)
+
+    @pl.when((lane != 0) | (group == 0))
+    def _():
+        edges[GROUP + 1] = jnp.zeros(edges.shape[1:], F32)
 
     @pl.when((lane != 0) | (group == 0))
     def _():
@@ -166,31 +169,43 @@
     weights[1].wait()
     stream = (tok.astype(F32) + dot(jnp.concatenate(mixed, axis=1), wof[...])).astype(BF16)
 
-    slots = capacity + TAIL
-    slot = iota((slots, length), 0)
-    gather = onehot(jnp.where(slot == capacity, -1, slot) == seg_lane[:slots])
+    slot = iota((capacity, length), 0)
+    gather = onehot(slot == seg_lane[:capacity])
+    edge_row = iota((TAIL, length), 0)
+    edge_seg = jnp.where(edge_row == 0, starts - 1, jnp.where(edge_row == 1, -1, starts - 2))
+    edge_gather = onehot((edge_row < 3) & (edge_seg == seg_lane[:TAIL]))
+    edge_sum = dot(edge_gather, stream)
+    edge_size = jnp.sum(edge_gather.astype(F32), axis=1, keepdims=True)
+    for r in range(3):
+        edges[lane, r, :, :width] = edge_sum[r:r + 1]
+        edges[lane, r, :, width:] = jnp.broadcast_to(edge_size[r:r + 1], (1, 128))
+    edge_copies = [
+        remote(edges.at[lane], edges.at[lane], edge_s.at[k], edge_r.at[lane], group * GROUP + peer)
+        for k, peer in enumerate(peers)
+    ]
+    down_copies = [
+        remote(edges.at[lane], edges.at[GROUP], edge_s.at[GROUP + j], edge_r.at[GROUP], lax.rem(me + n - GROUP + j, n))
+        for j in range(GROUP)
+    ]
+    up_copy = remote(edges.at[lane], edges.at[GROUP + 1], edge_s.at[GROUP - 1], edge_r.at[GROUP + 1], after)
+    sends_down = (lane == 0) & (group > 0)
+    sends_up = (lane == GROUP - 1) & (group < groups - 1)
+    for copy in edge_copies:
+        copy.start()
+
+    @pl.when(sends_down)
+    def _():
+        for copy in down_copies:
+            copy.start()
+
+    @pl.when(sends_up)
+    def _():
+        up_copy.start()
+
     partial = dot(gather, stream)
     sizes = jnp.sum(gather.astype(F32), axis=1, keepdims=True)
-    lead_out[:, :width] = partial[capacity:capacity + 8]
-    lead_out[:, width:] = jnp.broadcast_to(sizes[capacity:capacity + 8], (8, 128))
-    lead_copy = remote(lead_out, lead_in, lead_s, lead_r, before)
-
-    @pl.when(me > 0)
-    def _():
-        lead_copy.start()
-
-    slot_col = iota((capacity, 1), 0)
-    closing = jnp.where(slot_col == starts - 1, 1.0, 0.0)
+    pooled = (partial / jnp.maximum(sizes, 1.0)).astype(BF16)
     weights[2].wait()
-
-    @pl.when(me < n - 1)
-    def _():
-        remote(lead_out, lead_in, lead_s, lead_r, after).wait_recv()
-
-    lead = lead_in[0:1, :]
-    totals = partial[:capacity] + closing * lead[:, :width]
-    seg_sizes = sizes[:capacity] + closing * lead[:, width:width + 1]
-    pooled = (totals / jnp.maximum(seg_sizes, 1.0)).astype(BF16)
 
     short = dot(normalize(pooled), wqs[...]).astype(BF16)
     for j in range(GROUP):
@@ -203,15 +218,6 @@
     for copy in part_copies:
         copy.start()
     joined[lane] = parted[lane]
-
-    tail_row = iota((TAIL, capacity), 0)
-    tail_slot = iota((TAIL, capacity), 1)
-    rows_out[...] = dot(onehot((tail_row < 2) & (tail_slot == starts - 1 - tail_row)), pooled).astype(BF16)
-    rows_copy = remote(rows_out, rows_in, rows_s, rows_r, after)
-
-    @pl.when(me < n - 1)
-    def _():
-        rows_copy.start()
 
     for k, peer in enumerate(peers):
         remote(marks.at[lane], marks.at[peer], marks_s.at[k], marks_r.at[peer], group * GROUP + peer).wait_recv()
@@ -232,11 +238,36 @@
         owner_first = jnp.where(beyond, firsts[j], owner_first)
         owner_count = jnp.where(beyond, counts[j], owner_count)
     within = source & (capacity - 1)
-    compact = onehot((within < owner_count) & (within + owner_first == place))
+    compact = onehot((within < owner_count - 1) & (within + owner_first == place))
+
+    for k, peer in enumerate(peers):
+        remote(edges.at[lane], edges.at[peer], edge_s.at[k], edge_r.at[peer], group * GROUP + peer).wait_recv()
+
+    @pl.when(group < groups - 1)
+    def _():
+        remote(edges.at[lane], edges.at[GROUP], edge_s.at[0], edge_r.at[GROUP], after).wait_recv()
+
+    blank = jnp.zeros((TAIL - GROUP, width + 128), F32)
+    closed = jnp.concatenate([edges[j, 0] for j in range(GROUP)] + [blank], axis=0)
+    closed = closed + jnp.concatenate([edges[j + 1, 1] for j in range(GROUP)] + [blank], axis=0)
+    closed = (closed[:, :width] / jnp.maximum(closed[:, width:width + 1], 1.0)).astype(BF16)
+    closed = normalize(closed)
+    closed_rows = jnp.concatenate(
+        [
+            dot(closed, wqs[:, pl.ds(pl.multiple_of(part * INNER + lane * PAIR, PAIR), PAIR)])
+            for part in range(3)
+        ],
+        axis=1,
+    ).astype(BF16)
+    closed_id = iota((length, TAIL), 1)
+    closed_place = jnp.full((length, TAIL), -1, jnp.int32)
+    for j in range(GROUP):
+        closed_place = jnp.where(closed_id == j, firsts[j] + counts[j] - 1, closed_place)
+    closed_at = onehot(closed_place == iota((length, TAIL), 0))
 
     for k, peer in enumerate(peers):
         remote(parted.at[lane], joined.at[peer], part_s.at[k], part_r.at[peer], group * GROUP + peer).wait_recv()
-    rows = dot(compact, joined[...].reshape(GROUP * capacity, 3 * PAIR)).astype(BF16)
+    rows = (dot(compact, joined[...].reshape(GROUP * capacity, 3 * PAIR)) + dot(closed_at, closed_rows)).astype(BF16)
     kv_all[group] = rows[:, PAIR:]
 
     def kv_copy(other):
@@ -257,13 +288,17 @@
     row_total = jnp.sum(expsum, axis=-1, keepdims=True)
     running = dot(expsum.astype(BF16), rows[:, 2 * PAIR:])
 
-    @pl.when(me > 0)
-    def _():
-        remote(rows_out, rows_in, rows_s, rows_r, before).wait_recv()
-
+    @pl.when((lane == 0) & (group > 0))
+    def _():
+        remote(edges.at[lane], edges.at[GROUP + 1], edge_s.at[0], edge_r.at[GROUP + 1], before).wait_recv()
+
+    behind = jnp.where(lane == 0, GROUP + 1, lane - 1)
+    last = edges[behind, 0] + edges[lane, 1]
+    last_two = jnp.concatenate([last, edges[behind, 2], jnp.zeros((TAIL - 2, width + 128), F32)], axis=0)
+    last_two = (last_two[:, :width] / jnp.maximum(last_two[:, width:width + 1], 1.0)).astype(BF16)
     lift = onehot(iota((length, capacity), 1) == seg_sub[:, :capacity] - 1)
     lift_tail = onehot(iota((length, TAIL), 1) == -seg_sub[:, :TAIL])
-    pooled_lifted = dot(lift, pooled) + dot(lift_tail, rows_in[...])
+    pooled_lifted = dot(lift, pooled) + dot(lift_tail, last_two)
 
     def attend(step, carry):
         row_max, row_total, running = carry
@@ -321,13 +356,17 @@
     @pl.when(me < n - 1)
     def _():
         tok_copy.wait_send()
-        rows_copy.wait_send()
-
-    @pl.when(me > 0)
-    def _():
-        lead_copy.wait_send()
-
-    for copy in marks_copies + part_copies + mix_copies:
+
+    @pl.when(sends_down)
+    def _():
+        for copy in down_copies:
+            copy.wait_send()
+
+    @pl.when(sends_up)
+    def _():
+        up_copy.wait_send()
+
+    for copy in marks_copies + edge_copies + part_copies + mix_copies:
         copy.wait_send()
 
     def drain(other, carry):
@@ -362,21 +401,18 @@
             pltpu.VMEM(w_out_short.shape, BF16),
             pltpu.VMEM((length, width), BF16),
             pltpu.VMEM((2 * length, 2 * INNER), BF16),
-            pltpu.VMEM((8, width + 128), F32),
-            pltpu.VMEM((8, width + 128), F32),
+            pltpu.VMEM((GROUP + 2, 3, 1, width + 128), F32),
             pltpu.VMEM((GROUP, 8, length), jnp.int32),
             pltpu.VMEM((GROUP, capacity, 3 * PAIR), BF16),
             pltpu.VMEM((GROUP, capacity, 3 * PAIR), BF16),
-            pltpu.VMEM((TAIL, width), BF16),
-            pltpu.VMEM((TAIL, width), BF16),
             pltpu.VMEM((groups, length, 2 * PAIR), BF16),
             pltpu.VMEM((GROUP, length, PAIR), BF16),
             pltpu.VMEM((GROUP, TAIL, PAIR), BF16),
             dma((6,)),
-            dma, dma, dma, dma,
+            dma, dma,
+            dma((2 * GROUP,)), dma((GROUP + 2,)),
             dma((GROUP,)), dma((GROUP,)),
             dma((GROUP,)), dma((GROUP,)),
-            dma, dma,
             dma((groups,)), dma((groups,)),
             dma((GROUP,)), dma((GROUP,)),
             dma, dma((GROUP,)),

time: 31.1 us -> 29.4 us (0.945)
  Pallas kernels: 29.2 us -> 27.6 us
    pallas_call x1, Pallas kernels: 29.2 us -> 27.6 us  [shards(): pl.pallas_call(functools.partial(kernel, n), out_shape=jax.ShapeDtypeStru...]
where the time goes in v3:
time: 29.4 us; the launch traced here: 29.3 us
  Pallas kernels  27.6 us (94%)
  local copies, waits for them, and re-layouts  1.67 us (6%)
    pallas_call x1, Pallas kernels, shards(): pl.pallas_call(functools.partial(kernel, n), out_shape=jax.ShapeDtypeStru...  27.6 us
    unnamed x1, local copies, waits for them, and re-layouts  1.67 us

profile of v3, /device:TPU:25, one launch (start us, length us, event | category | flops | bytes accessed | tf_op | source)
XLA Modules:
  0.0 29.3 jit_solution(15805115973683332169)
XLA Ops:
  0.0 27.6 %shard_map.64 = bf16[128,1024]{1,0:T(8,128)(2,1)} custom-call(bf16[128,1024]{1,0:T(8,128)(2,1)} %tokens_hbm.1, s32[1,128]{1,0:T(1,128)} %bitcast.1, bf16[1024,1536]{1,0:T(8,128)(2,1)} %wqf_hbm.1, bf16[512,1024]{1,0:T(8,128)(2,1)} %wof_hbm.1, bf16[1024,1536]{1,0:T(8,128)(2,1)} %wqs_hbm.1, bf16[512,1024]{1,0:T(8,128)(2,1)} %wos_hbm.1), custom_call_target="tpu_custom_call" | custom-call | tf_op jit(solution)/shard_map/pallas_call | solution.py:390
  27.6 1.7 %copy.8 = bf16[128,1024]{1,0:T(8,128)(2,1)} copy(bf16[128,1024]{1,0:T(8,128)(2,1)} %shard_map.64) | data formatting | bytes 524288

commit v4 on v3

--- a/solution.py
+++ b/solution.py
@@ -56,7 +56,7 @@
     n, tokens_hbm, boundary_hbm, wqf_hbm, wof_hbm, wqs_hbm, wos_hbm, out,
     tokens, boundary, wqf, wof, wqs, wos, prev, kv_cat, edges, marks, parted, joined,
     kv_all, mix, mix_tail,
-    w_sem, tok_s, tok_r, edge_s, edge_r, marks_s, marks_r, part_s, part_r,
+    above, w_sem, tok_s, tok_r, edge_s, edge_r, marks_s, marks_r, part_s, part_r,
     kv_s, kv_r, mix_s, mix_r, mt_s, mt_r,
 ):
     length, width = tokens.shape
@@ -82,13 +82,38 @@
 
     barrier = pltpu.get_barrier_semaphore()
 
-    def greet(k, carry):
-        pl.semaphore_signal(
-            barrier, inc=1, device_id={"ctx": lax.rem(me + k, n)}, device_id_type=pl.DeviceIdType.MESH
-        )
-        return carry
-
-    lax.fori_loop(1, n, greet, 0)
+    def signal(semaphore, device):
+        pl.semaphore_signal(semaphore, inc=1, device_id={"ctx": device}, device_id_type=pl.DeviceIdType.MESH)
+
+    has_below = group > 0
+    has_above = group < groups - 1
+    for k in range(1, GROUP):
+        signal(barrier, group * GROUP + lax.rem(lane + k, GROUP))
+
+    @pl.when(has_above)
+    def _():
+        signal(barrier, me + GROUP)
+
+    @pl.when(has_below)
+    def _():
+        signal(barrier, me - GROUP)
+
+    @pl.when(has_above & (lane > 0))
+    def _():
+        signal(barrier, (group + 1) * GROUP)
+
+    @pl.when(has_below & (lane == 0))
+    def _():
+        for k in range(1, GROUP):
+            signal(barrier, me - k)
+
+    greeted = (
+        GROUP - 1
+        + jnp.where(has_above, 1, 0)
+        + jnp.where(has_below, 1, 0)
+        + jnp.where(has_above & (lane > 0), 1, 0)
+        + jnp.where(has_below & (lane == 0), GROUP - 1, 0)
+    )
     for i in (4, 5, 0, 1, 2, 3):
         weights[i].start()
 
@@ -125,7 +150,7 @@
     weights[4].wait()
     tok = tokens[...]
     normed = normalize(tok)
-    pl.semaphore_wait(barrier, n - 1)
+    pl.semaphore_wait(barrier, greeted)
 
     tok_copy = remote(tokens_hbm, prev, tok_s, tok_r, after)
 
@@ -144,6 +169,14 @@
     packed = dot(normed, wqf[...]).astype(BF16)
     queries = packed[:, :INNER]
     kv_cat[length:, :] = packed[:, INNER:]
+
+    @pl.when(has_below & has_above)
+    def _():
+        pl.semaphore_wait(above, 1)
+
+    @pl.when(has_below)
+    def _():
+        signal(above, me - GROUP)
 
     @pl.when(me > 0)
     def _():
@@ -269,6 +302,10 @@
         remote(parted.at[lane], joined.at[peer], part_s.at[k], part_r.at[peer], group * GROUP + peer).wait_recv()
     rows = (dot(compact, joined[...].reshape(GROUP * capacity, 3 * PAIR)) + dot(closed_at, closed_rows)).astype(BF16)
     kv_all[group] = rows[:, PAIR:]
+
+    @pl.when(has_above & (group == 0))
+    def _():
+        pl.semaphore_wait(above, 1)
 
     def kv_copy(other):
         return remote(kv_all.at[group], kv_all.at[group], kv_s.at[other], kv_r.at[group], other * GROUP + lane)
@@ -408,6 +445,7 @@
             pltpu.VMEM((groups, length, 2 * PAIR), BF16),
             pltpu.VMEM((GROUP, length, PAIR), BF16),
             pltpu.VMEM((GROUP, TAIL, PAIR), BF16),
+            pltpu.SemaphoreType.REGULAR,
             dma((6,)),
             dma, dma,
             dma((2 * GROUP,)), dma((GROUP + 2,)),

time: 29.4 us -> 27.7 us (0.942)
  Pallas kernels: 27.6 us -> 25.9 us
    pallas_call x1, Pallas kernels: 27.6 us -> 25.9 us  [shards(): pl.pallas_call(functools.partial(kernel, n), out_shape=jax.ShapeDtypeStru...]
where the time goes in v4:
time: 27.7 us; the launch traced here: 27.5 us
  Pallas kernels  25.9 us (94%)
  local copies, waits for them, and re-layouts  1.67 us (6%)
    pallas_call x1, Pallas kernels, shards(): pl.pallas_call(functools.partial(kernel, n), out_shape=jax.ShapeDtypeStru...  25.9 us
    unnamed x1, local copies, waits for them, and re-layouts  1.67 us

profile of v4, /device:TPU:25, one launch (start us, length us, event | category | flops | bytes accessed | tf_op | source)
XLA Modules:
  0.0 27.5 jit_solution(12910344404033424849)
XLA Ops:
  0.0 25.9 %shard_map.64 = bf16[128,1024]{1,0:T(8,128)(2,1)} custom-call(bf16[128,1024]{1,0:T(8,128)(2,1)} %tokens_hbm.1, s32[1,128]{1,0:T(1,128)} %bitcast.1, bf16[1024,1536]{1,0:T(8,128)(2,1)} %wqf_hbm.1, bf16[512,1024]{1,0:T(8,128)(2,1)} %wof_hbm.1, bf16[1024,1536]{1,0:T(8,128)(2,1)} %wqs_hbm.1, bf16[512,1024]{1,0:T(8,128)(2,1)} %wos_hbm.1), custom_call_target="tpu_custom_call" | custom-call | tf_op jit(solution)/shard_map/pallas_call | solution.py:427
  25.9 1.7 %copy.8 = bf16[128,1024]{1,0:T(8,128)(2,1)} copy(bf16[128,1024]{1,0:T(8,128)(2,1)} %shard_map.64) | data formatting | bytes 524288

commit v5 on v4

--- a/solution.py
+++ b/solution.py
@@ -114,7 +114,7 @@
         + jnp.where(has_above & (lane > 0), 1, 0)
         + jnp.where(has_below & (lane == 0), GROUP - 1, 0)
     )
-    for i in (4, 5, 0, 1, 2, 3):
+    for i in (4, 5, 0):
         weights[i].start()
 
     after = lax.rem(me + 1, n)
@@ -152,7 +152,7 @@
     normed = normalize(tok)
     pl.semaphore_wait(barrier, greeted)
 
-    tok_copy = remote(tokens_hbm, prev, tok_s, tok_r, after)
+    tok_copy = remote(tokens, prev, tok_s, tok_r, after)
 
     @pl.when(me < n - 1)
     def _():
@@ -164,6 +164,8 @@
     ]
     for copy in marks_copies:
         copy.start()
+    for i in (1, 2, 3):
+        weights[i].start()
 
     weights[0].wait()
     packed = dot(normed, wqf[...]).astype(BF16)
@@ -180,7 +182,7 @@
 
     @pl.when(me > 0)
     def _():
-        remote(tokens_hbm, prev, tok_s, tok_r, before).wait_recv()
+        remote(tokens, prev, tok_s, tok_r, before).wait_recv()
 
     kv_cat[:length, :] = dot(normalize(prev[...]), wqf[:, INNER:]).astype(BF16)
 
@@ -310,8 +312,8 @@
     def kv_copy(other):
         return remote(kv_all.at[group], kv_all.at[group], kv_s.at[other], kv_r.at[group], other * GROUP + lane)
 
-    def send(other, carry):
-        kv_copy(other).start()
+    def send(step, carry):
+        kv_copy(groups + group - step).start()
         return carry
 
     lax.fori_loop(group + 1, groups, send, 0)
@@ -456,7 +458,7 @@
             dma, dma((GROUP,)),
         ],
         compiler_params=pltpu.CompilerParams(
-            collective_id=0, has_side_effects=True, vmem_limit_bytes=60 * 1024 * 1024
+            collective_id=0, has_side_effects=True, vmem_limit_bytes=54850 * 1024
         ),
     )(tokens, boundary.reshape(1, length), w_qkv_full, w_out_full, w_qkv_short, w_out_short)
 

time: 27.7 us -> 26.5 us (0.957)
  the two profiles are of different devices: /device:TPU:25 before, /device:TPU:17 now
where the time goes in v5:
time: 26.5 us; the launch traced here: 26.4 us
  Pallas kernels  25 us (94%)
  local copies, waits for them, and re-layouts  1.36 us (5%)
    pallas_call x1, Pallas kernels, shards(): pl.pallas_call(functools.partial(kernel, n), out_shape=jax.ShapeDtypeStru...  25 us
    unnamed x3, local copies, waits for them, and re-layouts  1.36 us

profile of v5, /device:TPU:17, one launch (start us, length us, event | category | flops | bytes accessed | tf_op | source)
XLA Modules:
  0.0 26.4 jit_solution(6061187678585758997)
XLA Ops:
  0.0 0.0 copy-start
  0.0 0.7 %copy-done = s32[128]{0:T(128)S(1)} copy-done((s32[128]{0:T(128)S(1)}, s32[128]{0:T(128)}, u32[]{:S(2)}) %copy-start) | copy-done | bytes 536
  0.7 25.0 %shard_map.64 = bf16[128,1024]{1,0:T(8,128)(2,1)S(1)} custom-call(bf16[128,1024]{1,0:T(8,128)(2,1)} %tokens_hbm.1, s32[1,128]{1,0:T(1,128)S(1)} %bitcast.1, bf16[1024,1536]{1,0:T(8,128)(2,1)} %wqf_hbm.1, bf16[512,1024]{1,0:T(8,128)(2,1)} %wof_hbm.1, bf16[1024,1536]{1,0:T(8,128)(2,1)} %wqs_hbm.1, bf16[512,1024]{1,0:T(8,128)(2,1)} %wos_hbm.1), custom_call_target="tpu_custom_call" | custom-call | tf_op jit(solution)/shard_map/pallas_call | solution.py:429
  25.7 0.7 %copy.8 = bf16[128,1024]{1,0:T(8,128)(2,1)} copy(bf16[128,1024]{1,0:T(8,128)(2,1)S(1)} %shard_map.64) | data formatting | bytes 524288
Async XLA Ops:
  0.0 0.7 %copy-start = (s32[128]{0:T(128)S(1)}, s32[128]{0:T(128)}, u32[]{:S(2)}) copy-start(s32[128]{0:T(128)} %param.7) | copy-start | bytes 1540

commit v6 on v5

--- a/solution.py
+++ b/solution.py
@@ -119,7 +119,8 @@
 
     after = lax.rem(me + 1, n)
     before = lax.rem(me + n - 1, n)
-    peers = [lax.rem(lane + k, GROUP) for k in range(1, GROUP)]
+    odd = lax.rem(lane, 2)
+    peers = [lax.rem(lane + 2, GROUP), lax.rem(lane + 3 - 2 * odd, GROUP), lax.rem(lane + 1 + 2 * odd, GROUP)]
     weights[5].wait()
     bound = boundary[...]
     marks[lane] = jnp.broadcast_to(bound, (8, length))

time: 26.5 us -> 26.5 us (level)
  no operation moved by 1% of the time
where the time goes in v6:
time: 26.5 us; the launch traced here: 26.4 us
  Pallas kernels  25 us (94%)
  local copies, waits for them, and re-layouts  1.36 us (5%)
    pallas_call x1, Pallas kernels, shards(): pl.pallas_call(functools.partial(kernel, n), out_shape=jax.ShapeDtypeStru...  25 us
    unnamed x3, local copies, waits for them, and re-layouts  1.36 us

profile of v6, /device:TPU:17, one launch (start us, length us, event | category | flops | bytes accessed | tf_op | source)
XLA Modules:
  0.0 26.4 jit_solution(14262452314688793729)
XLA Ops:
  0.0 0.0 copy-start
  0.0 0.7 %copy-done = s32[128]{0:T(128)S(1)} copy-done((s32[128]{0:T(128)S(1)}, s32[128]{0:T(128)}, u32[]{:S(2)}) %copy-start) | copy-done | bytes 536
  0.7 25.0 %shard_map.64 = bf16[128,1024]{1,0:T(8,128)(2,1)S(1)} custom-call(bf16[128,1024]{1,0:T(8,128)(2,1)} %tokens_hbm.1, s32[1,128]{1,0:T(1,128)S(1)} %bitcast.1, bf16[1024,1536]{1,0:T(8,128)(2,1)} %wqf_hbm.1, bf16[512,1024]{1,0:T(8,128)(2,1)} %wof_hbm.1, bf16[1024,1536]{1,0:T(8,128)(2,1)} %wqs_hbm.1, bf16[512,1024]{1,0:T(8,128)(2,1)} %wos_hbm.1), custom_call_target="tpu_custom_call" | custom-call | tf_op jit(solution)/shard_map/pallas_call | solution.py:430
  25.7 0.7 %copy.8 = bf16[128,1024]{1,0:T(8,128)(2,1)} copy(bf16[128,1024]{1,0:T(8,128)(2,1)S(1)} %shard_map.64) | data formatting | bytes 524288
Async XLA Ops:
  0.0 0.7 %copy-start = (s32[128]{0:T(128)S(1)}, s32[128]{0:T(128)}, u32[]{:S(2)}) copy-start(s32[128]{0:T(128)} %param.7) | copy-start | bytes 1540
